TPU v7x, 128 devices: a whole 4x4x4 slice. The times are simulated.
128 devices in a mesh: hid: 8 (over z, x_hi), wid: 16 (over y, x_lo, core).
Axes of the slice: x: 4 (x_hi: 2, x_lo: 2; x = x_hi * 2 + x_lo), y: 4, z: 4, core: 2. Of those that a mesh axis runs over, the one named last changes fastest.
Arguments:
- spec_rows: int32 [1024, 2], replicated, may hold values from 0 to 2047, as said below
- readout: bfloat16 [2048, 8192], P(None, 'wid'), may hold values from -6 to 6
- gate_weight: bfloat16 [8192, 28672], P('wid', 'hid'), may hold values from -0.0625 to 0.0625
- up_weight: bfloat16 [8192, 28672], P('wid', 'hid'), may hold values from -0.0625 to 0.0625
- down_weight: bfloat16 [28672, 8192], P('hid', 'wid'), may hold values from -0.03125 to 0.03125
- gate_lo: float32 [28672], P('hid'), may hold values from -6 to 6
- gate_width: float32 [28672], P('hid'), may hold values from 0.5 to 4
- up_lo: float32 [28672], P('hid'), may hold values from -6 to 6
- up_width: float32 [28672], P('hid'), may hold values from 0.5 to 4
- flags: int32 [28672], P('hid'), may hold values 0 or 1
Outputs:
- input_coeffs: float32 [1024, 8192], P('hid', 'wid')
- offsets: float32 [1024], P('wid')
Inputs may be any that keep to these rules, and one draw needn't show every extreme that they name: `spec_rows`: each row names two different classes; every class is named by exactly one entry of one row.
All inputs are finite; a program needn't handle non-finite values. No bound on the sum of `flags` on one device may be relied on, other than what follows from the above.
Results may differ from a plain program's by a relative error of at most 0.0041.
Values may be sent and summed in bfloat16 or wider, within the bound.
A program may use at most 128 MiB of HBM per device.

v0:
```python
import jax
import jax.numpy as jnp
from jax import lax
from jax.sharding import PartitionSpec as P


def silu(value):
    return value / (1.0 + jnp.exp(-value))


def unit_tables(gate_lo, gate_width, up_lo, up_width, flags):
    gate_hi = gate_lo + gate_width
    up_hi = up_lo + up_width
    middle = 0.5 * (gate_lo + gate_hi)
    valley = jnp.clip(-1.2784645, gate_lo, gate_hi)
    silu_lo = silu(gate_lo)
    silu_hi = silu(gate_hi)
    s_low = jnp.minimum(jnp.minimum(silu_lo, silu_hi), silu(valley))
    s_high = jnp.maximum(silu_lo, silu_hi)
    slope = (silu_hi - silu_lo) / gate_width
    rest_a = silu_lo - slope * gate_lo
    rest_b = silu(middle) - slope * middle
    rest_c = silu(valley) - slope * valley
    b_low = jnp.minimum(jnp.minimum(rest_a, rest_b), rest_c)
    b_high = jnp.maximum(jnp.maximum(rest_a, rest_b), rest_c)
    second = flags == 1
    as_lower = jnp.where(second, up_hi, up_lo)
    au_lower = jnp.where(second, s_high, s_low)
    c_lower = jnp.where(second, -s_high * up_hi, -s_low * up_lo)
    as_upper = jnp.where(second, up_lo, up_hi)
    au_upper = jnp.where(second, s_high, s_low)
    c_upper = jnp.where(second, -s_high * up_lo, -s_low * up_hi)
    return (as_lower, au_lower, c_lower, as_upper, au_upper, c_upper, slope, b_low, b_high)


def relax(lam_h, tables):
    as_lower, au_lower, c_lower, as_upper, au_upper, c_upper, slope, b_low, b_high = tables
    plus = jnp.maximum(lam_h, 0.0)
    minus = jnp.minimum(lam_h, 0.0)
    lam_u = (plus * au_lower + minus * au_upper).astype(jnp.bfloat16)
    weight_s = plus * as_lower + minus * as_upper
    lam_g = (weight_s * slope).astype(jnp.bfloat16)
    terms = (
        plus * c_lower
        + minus * c_upper
        + jnp.maximum(weight_s, 0.0) * b_low
        + jnp.minimum(weight_s, 0.0) * b_high
    )
    return (lam_g, lam_u, jnp.sum(terms, axis=1))


def per_device(
    spec_rows,
    readout,
    gate_weight,
    up_weight,
    down_weight,
    gate_lo,
    gate_width,
    up_lo,
    up_width,
    flags,
):
    dims = (((1,), (1,)), ((), ()))
    total_rows = spec_rows.shape[0]
    target = jnp.take(readout, spec_rows[:, 0], axis=0).astype(jnp.float32)
    rival = jnp.take(readout, spec_rows[:, 1], axis=0).astype(jnp.float32)
    lam = (target - rival).astype(jnp.bfloat16)
    tables = unit_tables(gate_lo, gate_width, up_lo, up_width, flags)
    lam_h = lax.psum_scatter(
        lax.dot_general(lam, down_weight, dims, preferred_element_type=jnp.float32),
        "wid",
        scatter_dimension=0,
        tiled=True,
    )
    lam_g, lam_u, partial_offsets = relax(lam_h, tables)
    lam_g, lam_u = (
        lax.all_gather(lam_g, "wid", axis=0, tiled=True),
        lax.all_gather(lam_u, "wid", axis=0, tiled=True),
    )
    offsets = lax.psum(partial_offsets, "hid")
    hidden_share = total_rows // lax.axis_size("hid")
    through_gate = lax.dot_general(lam_g, gate_weight, dims, preferred_element_type=jnp.float32)
    summed = lax.psum_scatter(
        through_gate + lax.dot_general(lam_u, up_weight, dims, preferred_element_type=jnp.float32),
        "hid",
        scatter_dimension=0,
        tiled=True,
    )
    own_rows = lax.dynamic_slice_in_dim(lam, lax.axis_index("hid") * hidden_share, hidden_share, 0)
    input_coeffs = own_rows.astype(jnp.float32) + summed
    return (input_coeffs, offsets)


def solution(mesh):
    placed = (
        P(),
        P(None, "wid"),
        P("wid", "hid"),
        P("wid", "hid"),
        P("hid", "wid"),
        P("hid"),
        P("hid"),
        P("hid"),
        P("hid"),
        P("hid"),
    )
    return jax.shard_map(
        per_device,
        mesh=mesh,
        in_specs=placed,
        out_specs=(P("hid", "wid"), P("wid")),
        check_vma=False,
    )
```

profile of v0, /device:TPU:0, one launch (start us, length us, event | category | flops | bytes accessed | tf_op | source)
XLA Modules:
  0.0 387.4 jit_solution(4655205852314555495)
XLA Ops:
  7.2 0.0 copy-start
  7.2 0.0 reduce-scatter.3.cloned.1.call-start
  7.2 0.9 fusion.2
  8.1 0.7 copy-done
  8.8 4.0 %gather_fusion = bf16[1024,512]{1,0:T(8,128)(2,1)S(1)} fusion(bf16[2048,512]{1,0:T(8,128)(2,1)S(1)} %copy-done, s32[1024]{0:T(1024)S(1)} %fusion), kind=kCustom, calls=%fused_computation.clone | custom fusion | bytes 2101248 | tf_op jit(solution)/shard_map/jit(_take)/gather | solution.py:66
  12.8 5.1 %gather_fusion.1 = bf16[1024,512]{1,0:T(8,128)(2,1)} fusion(bf16[2048,512]{1,0:T(8,128)(2,1)S(1)} %copy-done, s32[1024]{0:T(1024)S(1)} %fusion.1), kind=kCustom, calls=%fused_computation.1.clone | custom fusion | bytes 2101248 | tf_op jit(solution)/shard_map/jit(_take)/gather | solution.py:67
  17.8 1.8 subtract_convert_fusion
  19.6 0.0 copy-start.1
  19.6 1.0 copy-done.1
  20.6 9.4 %fusion.3 = f32[1024,3584]{1,0:T(8,128)} fusion(bf16[1024,512]{1,0:T(8,128)(2,1)S(1)} %subtract_convert_fusion, bf16[3584,512]{1,0:T(8,128)(2,1)} %param.16), kind=kOutput, calls=%fused_computation.33 | convolution fusion | flops 3758096384 | bytes 19398656 | tf_op jit(solution)/shard_map/dot_general | solution.py:71
  30.0 0.0 copy-start.2
  30.0 0.0 copy-start.3
  30.0 0.0 copy-start.4
  30.0 0.0 copy-start.5
  30.0 0.0 copy-start.6
  30.0 0.0 reduce-scatter.3.cloned.1.call-update
  30.0 0.0 all-gather.3.cloned.1.call-start
  30.1 0.6 copy-done.2
  30.7 0.0 copy-done.3
  30.7 0.0 copy-done.4
  30.7 0.0 copy-done.5
  30.7 0.0 copy-done.6
  30.8 163.0 %reduce-scatter.3.cloned.1.call-done = f32[64,3584]{1,0:T(8,128)} async-done(((f32[1024,3584]{1,0:T(8,128)}), f32[64,3584]{1,0:T(8,128)}) %reduce-scatter.3.cloned.1.call-update) | async-done | bytes 917520 | tf_op jit(solution)/shard_map/reduce_scatter | solution.py:70
  193.8 2.8 add_reduce_fusion
  196.6 0.0 all-gather.3.cloned.1.call-update
  196.7 0.0 all-gather.5.cloned.1.call-start
  196.7 0.7 all-gather.5.cloned.1.call-update
  197.4 0.0 reduce-scatter.5.cloned.1.call-start
  197.4 45.3 %all-gather.3.cloned.1.call-done = bf16[1024,3584]{1,0:T(8,128)(2,1)} async-done(((bf16[64,3584]{1,0:T(8,128)(2,1)}), bf16[1024,3584]{1,0:T(8,128)(2,1)}) %all-gather.3.cloned.1.call-update) | async-done | bytes 7340048 | tf_op jit(solution)/shard_map/all_gather | solution.py:78
  242.8 9.4 %fusion.4 = f32[1024,512]{1,0:T(8,128)} fusion(bf16[1024,3584]{1,0:T(8,128)(2,1)} %all-gather.3.cloned.1.call-done, bf16[512,3584]{1,0:T(8,128)(2,1)} %param.14), kind=kOutput, calls=%fused_computation.34 | convolution fusion | flops 3758096384 | bytes 13107200 | tf_op jit(solution)/shard_map/dot_general | solution.py:83
  252.2 40.5 %all-gather.5.cloned.1.call-done = bf16[1024,3584]{1,0:T(8,128)(2,1)} async-done(((bf16[64,3584]{1,0:T(8,128)(2,1)}), bf16[1024,3584]{1,0:T(8,128)(2,1)}) %all-gather.5.cloned.1.call-update) | async-done | bytes 7340048 | tf_op jit(solution)/shard_map/all_gather | solution.py:79
  292.6 10.1 %convolution_add_fusion = f32[1024,512]{1,0:T(8,128)} fusion(f32[1024,512]{1,0:T(8,128)} %fusion.4, bf16[1024,3584]{1,0:T(8,128)(2,1)} %all-gather.5.cloned.1.call-done, bf16[512,3584]{1,0:T(8,128)(2,1)} %param.15), kind=kOutput, calls=%fused_computation.3 | convolution fusion | flops 3758620672 | bytes 15204352 | tf_op jit(solution)/shard_map/dot_general | solution.py:85
  302.7 0.0 reduce-scatter.5.cloned.1.call-update
  302.7 25.0 %psum.7 = f32[64]{0:T(128)} all-reduce(f32[64]{0:T(128)S(1)} %get-tuple-element.5), channel_id=1, replica_groups=mesh['hid'=8,'wid'=16] {'hid'}, use_global_device_ids=true, to_apply=%region_3.5 | all-reduce | flops 64 | bytes 512 | tf_op jit(solution)/shard_map/psum | solution.py:81
  327.8 51.3 %reduce-scatter.5.cloned.1.call-done = f32[128,512]{1,0:T(8,128)} async-done(((f32[1024,512]{1,0:T(8,128)}), f32[128,512]{1,0:T(8,128)}) %reduce-scatter.5.cloned.1.call-update) | async-done | bytes 262160 | tf_op jit(solution)/shard_map/reduce_scatter | solution.py:84
  379.1 1.7 convert_add_fusion
  (5 shorter events, 0.1 us)
Async XLA Ops:
  7.2 1.6 copy-start
  7.2 186.6 %reduce-scatter.3.cloned.1.call-start = ((), (), s32[]{:S(2)}) async-start(), calls=%async_computation.2 | async-start | bytes 15597568 | tf_op jit(solution)/shard_map/reduce_scatter | solution.py:70
  19.6 1.0 copy-start.1
  30.0 0.7 copy-start.2
  30.0 0.7 copy-start.3
  30.0 0.7 copy-start.4
  30.0 0.8 copy-start.5
  30.0 0.8 copy-start.6
  30.0 212.7 %all-gather.3.cloned.1.call-start = ((), (), s32[]{:S(2)}) async-start(), calls=%async_computation.3 | async-start | bytes 7798784 | tf_op jit(solution)/shard_map/all_gather | solution.py:78
  196.7 96.0 %all-gather.5.cloned.1.call-start = ((), (), s32[]{:S(2)}) async-start(), calls=%async_computation.4 | async-start | bytes 7798784 | tf_op jit(solution)/shard_map/all_gather | solution.py:79
  197.4 181.7 %reduce-scatter.5.cloned.1.call-start = ((), (), s32[]{:S(2)}) async-start(), calls=%async_computation.5 | async-start | bytes 2359296 | tf_op jit(solution)/shard_map/reduce_scatter | solution.py:84
Sparse Core Ops, SparseCore 0:
  30.1 163.6 reduce-scatter.2
  196.8 45.9 all-gather.2
  244.5 48.1 all-gather.4
  302.9 76.2 reduce-scatter.4
where the time goes:
time: 388 us; the launch traced here: 387 us
  waiting for transfers between devices  301 us (78%)
  matrix products  28.8 us (7%)
  blocking collectives  25 us (6%)
  between operations  13.9 us (4%)
  local copies, waits for them, and re-layouts  12.2 us (3%)
  other arithmetic  6.39 us (2%)
    reduce_scatter x1, waiting for transfers between devices, per_device(): lax.psum_scatter(lax.dot_general(lam, down_weight, dims, preferred_elemen...  163 us
    reduce_scatter x1, waiting for transfers between devices, per_device(): lax.psum_scatter(through_gate + lax.dot_general(lam_u, up_weight, dims, p...  51.3 us
    all_gather x1, waiting for transfers between devices, per_device(): lax.all_gather(lam_g, 'wid', axis=0, tiled=True)  45.3 us
    all_gather x1, waiting for transfers between devices, per_device(): lax.all_gather(lam_u, 'wid', axis=0, tiled=True)  40.5 us
    psum x1, blocking collectives, per_device(): offsets = lax.psum(partial_offsets, 'hid')  25 us
    dot_general x1, matrix products, per_device(): lax.dot_general(lam_u, up_weight, dims, preferred_element_type=jnp.float32)  10.1 us
    dot_general x1, matrix products, per_device(): lax.dot_general(lam_g, gate_weight, dims, preferred_element_type=jnp.floa...  9.39 us
    dot_general x1, matrix products, per_device(): lax.dot_general(lam, down_weight, dims, preferred_element_type=jnp.float32)  9.38 us
  transfers between devices with their start and end apart: 4, of which 4 were waited for; matrix products, arithmetic and copies ran while one was open for 2% of the time, Pallas kernels for 0%

commit v1 on v0

v1 whole, which is shorter than its diff:
```python
import functools

import jax
import jax.numpy as jnp
from jax import lax
from jax.experimental import pallas as pl
from jax.experimental.pallas import tpu as pltpu
from jax.sharding import PartitionSpec as P

MESH = pl.DeviceIdType.MESH
F32 = jnp.float32
BF16 = jnp.bfloat16
NT = (((1,), (1,)), ((), ()))

CHUNKS = 4
OWN = 32
HALF = OWN // 2


def silu(value):
    return value / (1.0 + jnp.exp(-value))


def unit_tables(gate_lo, gate_width, up_lo, up_width, flags):
    gate_hi = gate_lo + gate_width
    up_hi = up_lo + up_width
    middle = 0.5 * (gate_lo + gate_hi)
    valley = jnp.clip(-1.2784645, gate_lo, gate_hi)
    silu_lo = silu(gate_lo)
    silu_hi = silu(gate_hi)
    silu_valley = silu(valley)
    s_low = jnp.minimum(jnp.minimum(silu_lo, silu_hi), silu_valley)
    s_high = jnp.maximum(silu_lo, silu_hi)
    slope = (silu_hi - silu_lo) / gate_width
    rest_a = silu_lo - slope * gate_lo
    rest_b = silu(middle) - slope * middle
    rest_c = silu_valley - slope * valley
    b_low = jnp.minimum(jnp.minimum(rest_a, rest_b), rest_c)
    b_high = jnp.maximum(jnp.maximum(rest_a, rest_b), rest_c)
    second = flags == 1
    as_lower = jnp.where(second, up_hi, up_lo)
    as_upper = jnp.where(second, up_lo, up_hi)
    au = jnp.where(second, s_high, s_low)
    kp = jnp.maximum(as_lower, 0.0) * b_low + jnp.minimum(as_lower, 0.0) * b_high - au * as_lower
    kn = jnp.minimum(as_upper, 0.0) * b_low + jnp.maximum(as_upper, 0.0) * b_high - au * as_upper
    return au, as_lower * slope, as_upper * slope, kp, kn


STEPS = {
    "lam": 0.0,
    "down": 1.5,
    "x1": 7.0,
    "y1": 7.1,
    "x2": 10.0,
    "y2": 10.1,
    "x3": 13.0,
    "y3": 13.1,
    "gx1": 16.0,
    "gy1": 16.1,
    "gx2": 19.0,
    "gy2": 19.1,
    "gx3": 22.0,
    "gy3": 22.1,
    "mm": 24.0,
    "z1": 28.0,
    "z2": 31.0,
    "out": 34.0,
}
STARTS = (0.0, 4.0, 14.0, 25.0)


def kernel(
    spec, readout, gate, up, down, gate_lo, gate_width, up_lo, up_width, flags,
    out, off,
    ro, wp, wn, dn, ds, oh, lam, lams, tab,
    px, py, x1s, x1r, xps, xpr, xqs, xqr, yps, ypr, yqs, yqr, yxs, yxr,
    lx, ly, acc, zps, zpr, zqs, zqr, hs, hr, oacc, obs, obr,
    lsem, ssem, rsem,
):
    hid, wid = lax.axis_index("hid"), lax.axis_index("wid")
    z, xh = hid // 2, hid % 2
    y, a, c = wid // 4, (wid // 2) % 2, wid % 2
    half = dn.shape[0]
    cx, cy = px.shape[-1], py.shape[-1]
    d_own = dn.shape[1]
    rows = CHUNKS * 0 + 8 * OWN
    yu, yd, yo = (y + 1) % 4, (y + 3) % 4, (y + 2) % 4
    zu, zd, zo = (z + 1) % 4, (z + 3) % 4, (z + 2) % 4

    def at(z_, xh_, y_, a_, c_):
        return (z_ * 2 + xh_, (y_ * 2 + a_) * 2 + c_)

    up_y, down_y = at(z, xh, yu, a, c), at(z, xh, yd, a, c)
    other_x = at(z, xh, y, 1 - a, c)
    twin = at(z, xh, y, a, 1 - c)
    up_z, down_z = at(zu, xh, y, a, c), at(zd, xh, y, a, c)
    other_h = at(z, 1 - xh, y, a, c)

    barrier = pltpu.get_barrier_semaphore()
    for device in (up_y, down_y, other_x, twin, up_z, down_z, other_h):
        pl.semaphore_signal(barrier, inc=1, device_id=device, device_id_type=MESH)

    load_ro = pltpu.make_async_copy(readout, ro, lsem.at[0])
    load_ro.start()
    my_half = pl.multiple_of(c * half, half)
    its_half = pl.multiple_of((1 - c) * half, half)
    load_dx = pltpu.make_async_copy(down.at[pl.ds(my_half, cx)], dn.at[pl.ds(0, cx)], lsem.at[1])
    load_dy = pltpu.make_async_copy(
        down.at[pl.ds(pl.multiple_of(my_half + cx, 256), cy)], dn.at[pl.ds(cx, cy)], lsem.at[2]
    )
    load_dx.start()
    load_dy.start()
    load_up = pltpu.make_async_copy(up, wp, lsem.at[3])
    load_gate = pltpu.make_async_copy(gate, wn, lsem.at[4])
    load_up.start()
    load_gate.start()

    copies = {}
    index = {}

    def send(name, r, src, dst, device):
        k = index.setdefault(name, len(index))
        copy = pltpu.make_async_remote_copy(
            src_ref=src, dst_ref=dst, send_sem=ssem.at[k, r], recv_sem=rsem.at[k, r],
            device_id=device, device_id_type=MESH,
        )
        copy.start()
        copies[name, r] = copy

    def arrive(name, r):
        copies[name, r].wait_recv()

    for k, table in enumerate(
        unit_tables(gate_lo[...], gate_width[...], up_lo[...], up_width[...], flags[...])
    ):
        tab[k, 0 : table.shape[0], :] = table

    def lam_rows(r):
        def group(g, carry):
            a_, y_, co = g // 8, (g // 2) % 4, g % 2
            start = pl.multiple_of((y_ * 2 + a_) * 128 + co * 64 + r * 16, 16)
            pair = spec[pl.ds(start, 16), :]
            classes = lax.broadcasted_iota(jnp.int32, (16, ro.shape[0]), 1)
            picked = jnp.where(classes == pair[:, 0:1], 1.0, 0.0) - jnp.where(classes == pair[:, 1:2], 1.0, 0.0)
            oh[pl.ds(pl.multiple_of(g * 16, 16), 16), :] = picked.astype(BF16)
            return carry

        lax.fori_loop(0, 16, group, 0)
        lam[r] = jnp.dot(oh[...], ro[...], preferred_element_type=F32).astype(BF16)

    def tree_first(stage, get, u, d, o):
        lead = (slice(None),) * (len(stage.shape) - 3)
        stage[(0, *lead, slice(0, HALF))] = get(o, 0).astype(stage.dtype)
        stage[(0, *lead, slice(HALF, OWN))] = get(u, 1).astype(stage.dtype)
        stage[(1, *lead, slice(0, HALF))] = get(d, 0).astype(stage.dtype)
        stage[(1, *lead, slice(HALF, OWN))] = get(o, 1).astype(stage.dtype)

    def tree_second(stage, came, get, u, d):
        lead = (slice(None),) * (len(came.shape) - 3)
        stage[0] = (get(u, 0) + came[(0, *lead, slice(0, HALF))].astype(F32)).astype(stage.dtype)
        stage[1] = (get(d, 1) + came[(1, *lead, slice(HALF, OWN))].astype(F32)).astype(stage.dtype)

    def tree_last(came, second, get, own):
        lead = (slice(None),) * (len(came.shape) - 3)
        low = get(own, 0) + came[(1, *lead, slice(0, HALF))].astype(F32) + second[0].astype(F32)
        high = get(own, 1) + came[(0, *lead, slice(HALF, OWN))].astype(F32) + second[1].astype(F32)
        return low, high

    def halves(h):
        return slice(h * HALF, (h + 1) * HALF)

    def get_x(r):
        return lambda y_, h: px[r, a * 4 + y_, halves(h)]

    def get_y(r):
        return lambda y_, h: py[r, :, y_, halves(h)]

    def get_z(r):
        return lambda z_, h: acc[r, :, z_, halves(h)]

    def constant_terms(r, h, value, first):
        blocks = value.shape[-1] // 128
        total = jnp.zeros((HALF, 128), F32)
        for j in range(blocks):
            row = c * (half // 128) + first + j
            part = value[:, j * 128 : (j + 1) * 128]
            total = total + jnp.maximum(part, 0.0) * tab[3, pl.ds(row, 1), :]
            total = total + jnp.minimum(part, 0.0) * tab[4, pl.ds(row, 1), :]
        if first == 0:
            oacc[h, r] = total
        else:
            oacc[h, r] += total

    def step_lam(r):
        if r == 0:
            load_ro.wait()
        lam_rows(r)
        if r == 0:
            pl.semaphore_wait(barrier, 7)
            send("lam", r, lam.at[r], lams.at[r], twin)
            send("dx", 0, down.at[pl.ds(its_half, cx)], ds.at[pl.ds(0, cx)], twin)
            send("dy", 0, down.at[pl.ds(pl.multiple_of(its_half + cx, 256), cy)], ds.at[pl.ds(cx, cy)], twin)
        else:
            send("lam", r, lam.at[r], lams.at[r], twin)

    def times_down(r, first, count, target):
        def block(n, carry):
            units = pl.ds(pl.multiple_of(first + n * 256, 256), 256)
            part = lax.dot_general(lam[r], dn[units, :], NT, preferred_element_type=F32)
            part = part + lax.dot_general(lams[r], ds[units, :], NT, preferred_element_type=F32)
            target(pl.ds(pl.multiple_of(n * 256, 256), 256), part)
            return carry

        lax.fori_loop(0, count // 256, block, 0)

    def step_down(r):
        arrive("lam", r)
        if r == 0:
            load_dx.wait()
            arrive("dx", 0)

        def to_x(columns, part):
            px[r, :, :, columns] = part.reshape(8, OWN, 256)

        def to_y(columns, part):
            py[r, :, :, :, columns] = part.reshape(2, 4, OWN, 256)

        times_down(r, 0, cx, to_x)
        x1s[r] = px[r, pl.ds((1 - a) * 4, 4)].astype(BF16)
        send("x1", r, x1s.at[r], x1r.at[r], other_x)
        if r == 0:
            load_dy.wait()
            arrive("dy", 0)
        times_down(r, cx, cy, to_y)
        tree_first(yps.at[r], get_y(r), yu, yd, yo)
        send("yu1", r, yps.at[r, 0], ypr.at[r, 0], up_y)
        send("yd1", r, yps.at[r, 1], ypr.at[r, 1], down_y)

    def step_x1(r):
        arrive("x1", r)
        mine = pl.ds(a * 4, 4)
        px[r, mine] += x1r[r].astype(F32)
        tree_first(xps.at[r], get_x(r), yu, yd, yo)
        send("xu1", r, xps.at[r, 0], xpr.at[r, 0], up_y)
        send("xd1", r, xps.at[r, 1], xpr.at[r, 1], down_y)

    def step_y1(r):
        arrive("yu1", r)
        arrive("yd1", r)
        tree_second(yqs.at[r], ypr.at[r], get_y(r), yu, yd)
        send("yu2", r, yqs.at[r, 0], yqr.at[r, 0], up_y)
        send("yd2", r, yqs.at[r, 1], yqr.at[r, 1], down_y)

    def step_x2(r):
        arrive("xu1", r)
        arrive("xd1", r)
        tree_second(xqs.at[r], xpr.at[r], get_x(r), yu, yd)
        send("xu2", r, xqs.at[r, 0], xqr.at[r, 0], up_y)
        send("xd2", r, xqs.at[r, 1], xqr.at[r, 1], down_y)

    def step_y2(r):
        arrive("yu2", r)
        arrive("yd2", r)
        low, high = tree_last(ypr.at[r], yqr.at[r], get_y(r), y)
        py[r, :, y, halves(0)] = low
        py[r, :, y, halves(1)] = high
        yxs[r] = py[r, 1 - a, y].astype(BF16)
        send("yx", r, yxs.at[r], yxr.at[r], other_x)

    def step_x3(r):
        arrive("xu2", r)
        arrive("xd2", r)
        for h, value in enumerate(tree_last(xpr.at[r], xqr.at[r], get_x(r), y)):
            lx[r, c, a, y, halves(h)] = value.astype(BF16)
            constant_terms(r, h, value, 0)
        block = lx.at[r, c, a, y]
        send("gxu1", r, block, block, up_y)
        send("gxd1", r, block, block, down_y)
        send("gxx0", r, block, block, other_x)

    def step_y3(r):
        arrive("yx", r)
        for h in range(2):
            value = py[r, a, y, halves(h)] + yxr[r, halves(h)].astype(F32)
            ly[r, c, a, y, halves(h)] = value.astype(BF16)
            constant_terms(r, h, value, cx // 128)
        block = ly.at[r, c, a, y]
        send("gyx", r, block, block, other_x)
        send("gyu1", r, block, block, up_y)
        send("gyd1", r, block, block, down_y)

    def step_gx1(r):
        arrive("gxu1", r)
        arrive("gxd1", r)
        below = lx.at[r, c, a, yd, halves(0)]
        above = lx.at[r, c, a, yu, halves(1)]
        send("gxu2", r, below, below, up_y)
        send("gxd2", r, above, above, down_y)
        for name, y_ in (("gxx1", yu), ("gxx2", yd)):
            block = lx.at[r, c, a, y_]
            send(name, r, block, block, other_x)

    def step_gy1(r):
        arrive("gyx", r)
        block = ly.at[r, c, 1 - a, y]
        send("gyu1b", r, block, block, up_y)
        send("gyd1b", r, block, block, down_y)

    def step_gx2(r):
        arrive("gxu2", r)
        arrive("gxd2", r)
        block = lx.at[r, c, a, yo]
        send("gxx3", r, block, block, other_x)
        block = lx.at[r, c, a]
        send("tx0", r, block, block, twin)

    def step_gy2(r):
        for name in ("gyu1", "gyd1", "gyu1b", "gyd1b"):
            arrive(name, r)
        below = ly.at[r, c, :, yd, halves(0)]
        above = ly.at[r, c, :, yu, halves(1)]
        send("gyu2", r, below, below, up_y)
        send("gyd2", r, above, above, down_y)

    def step_gx3(r):
        for k in range(4):
            arrive("gxx%d" % k, r)
        block = lx.at[r, c, 1 - a]
        send("tx1", r, block, block, twin)

    def step_gy3(r):
        arrive("gyu2", r)
        arrive("gyd2", r)
        block = ly.at[r, c]
        send("ty", r, block, block, twin)

    def times_weights(r, cc, add):
        base = cc * half
        columns_x = pl.ds(pl.multiple_of(base, 256), cx)
        columns_y = pl.ds(pl.multiple_of(base + cx, 256), cy)

        def block(n, carry):
            units = pl.ds(pl.multiple_of(n * 256, 256), 256)
            total = None
            for ref, columns in ((lx, columns_x), (ly, columns_y)):
                value = ref[r, cc].reshape(rows, columns.size)
                for part, weight in ((jnp.maximum(value, 0), wp), (jnp.minimum(value, 0), wn)):
                    term = lax.dot_general(part, weight[units, columns], NT, preferred_element_type=F32)
                    total = term if total is None else total + term
            total = total.reshape(2, 4, OWN, 256)
            if add:
                acc[r, :, :, :, units] += total
            else:
                acc[r, :, :, :, units] = total
            return carry

        lax.fori_loop(0, d_own // 256, block, 0)

    def step_mm(r):
        times_weights(r, c, False)
        arrive("tx0", r)
        arrive("tx1", r)
        arrive("ty", r)
        times_weights(r, 1 - c, True)
        tree_first(zps.at[r], get_z(r), zu, zd, zo)
        send("zu1", r, zps.at[r, 0], zpr.at[r, 0], up_z)
        send("zd1", r, zps.at[r, 1], zpr.at[r, 1], down_z)

    def step_z1(r):
        arrive("zu1", r)
        arrive("zd1", r)
        tree_second(zqs.at[r], zpr.at[r], get_z(r), zu, zd)
        send("zu2", r, zqs.at[r, 0], zqr.at[r, 0], up_z)
        send("zd2", r, zqs.at[r, 1], zqr.at[r, 1], down_z)

    def step_z2(r):
        arrive("zu2", r)
        arrive("zd2", r)
        low, high = tree_last(zpr.at[r], zqr.at[r], get_z(r), z)
        acc[r, :, z, halves(0)] = low
        acc[r, :, z, halves(1)] = high
        hs[r] = acc[r, 1 - xh, z]
        send("h", r, hs.at[r], hr.at[r], other_h)

    def step_out(r):
        arrive("h", r)
        first = (xh * 4 + z) * OWN
        for h in range(2):
            own = lam[r, pl.ds(pl.multiple_of(first + h * HALF, HALF), HALF), :].astype(F32)
            out[h * 64 + r * HALF : h * 64 + (r + 1) * HALF, :] = own + acc[r, xh, z, halves(h)] + hr[r, halves(h)]

    def weights(k):
        if k == 0:
            load_up.wait()
            load_gate.wait()

        def block(j, carry):
            columns = pl.ds(pl.multiple_of(j * 128, 128), 128)
            scaled = wp[:, columns].astype(F32) * tab[0, pl.ds(j, 1), :]
            gates = wn[:, columns].astype(F32)
            wp[:, columns] = (scaled + gates * tab[1, pl.ds(j, 1), :]).astype(BF16)
            wn[:, columns] = (scaled + gates * tab[2, pl.ds(j, 1), :]).astype(BF16)
            return carry

        count = wp.shape[1] // 128 // 2
        lax.fori_loop(k * count, (k + 1) * count, block, 0)

    partners = (
        twin,
        at(z + 1 - 2 * (z % 2), xh, y, a, c),
        at(3 - z, xh, y, a, c),
        other_h,
    )

    def offset_start():
        obs[0] = jnp.broadcast_to(jnp.sum(oacc[...].reshape(128, 128).T, axis=0, keepdims=True), (8, 128))
        send("o", 0, obs.at[0], obr.at[0], partners[0])

    def offset_step(k):
        arrive("o", k - 1)
        if k < 4:
            obs[k] = obs[k - 1] + obr[k - 1]
            send("o", k, obs.at[k], obr.at[k], partners[k])
        else:
            total = obs[k - 1] + obr[k - 1]
            off[...] = jnp.where(c == 0, total[0:1, 0:64], total[0:1, 64:128])

    table = dict(
        lam=step_lam, down=step_down, x1=step_x1, y1=step_y1, x2=step_x2, y2=step_y2, x3=step_x3, y3=step_y3,
        gx1=step_gx1, gy1=step_gy1, gx2=step_gx2, gy2=step_gy2, gx3=step_gx3, gy3=step_gy3,
        mm=step_mm, z1=step_z1, z2=step_z2, out=step_out,
    )
    plan = [
        (start + when, functools.partial(table[name], r))
        for r, start in enumerate(STARTS)
        for name, when in STEPS.items()
    ]
    plan.append((STARTS[1] + 2.0, functools.partial(weights, 0)))
    plan.append((STARTS[1] + 6.05, functools.partial(weights, 1)))
    last = STARTS[-1]
    plan.append((last + 13.2, offset_start))
    for k, when in ((1, 19.2), (2, 22.2), (3, 28.2), (4, 31.2)):
        plan.append((last + when, functools.partial(offset_step, k)))
    for _, step in sorted(plan, key=lambda item: item[0]):
        step()
    for copy in copies.values():
        copy.wait_send()


def per_device(
    spec_rows, readout, gate_weight, up_weight, down_weight, gate_lo, gate_width, up_lo, up_width, flags
):
    d_own = readout.shape[1]
    units = down_weight.shape[0]
    half = units // 2
    cx = 768
    cy = half - cx
    rows = 8 * OWN
    r = CHUNKS
    lanes = [value.reshape(units // 128, 128) for value in (gate_lo, gate_width, up_lo, up_width, flags)]
    vm = pltpu.VMEM
    scratch = [
        vm((readout.shape[0], d_own), BF16),
        vm((d_own, units), BF16),
        vm((d_own, units), BF16),
        vm((half, d_own), BF16),
        vm((half, d_own), BF16),
        vm((rows, readout.shape[0]), BF16),
        vm((r, rows, d_own), BF16),
        vm((r, rows, d_own), BF16),
        vm((5, 32, 128), F32),
        vm((r, 8, OWN, cx), F32),
        vm((r, 2, 4, OWN, cy), F32),
        vm((r, 4, OWN, cx), BF16),
        vm((r, 4, OWN, cx), BF16),
        vm((r, 2, OWN, cx), BF16),
        vm((r, 2, OWN, cx), BF16),
        vm((r, 2, HALF, cx), BF16),
        vm((r, 2, HALF, cx), BF16),
        vm((r, 2, 2, OWN, cy), BF16),
        vm((r, 2, 2, OWN, cy), BF16),
        vm((r, 2, 2, HALF, cy), BF16),
        vm((r, 2, 2, HALF, cy), BF16),
        vm((r, OWN, cy), BF16),
        vm((r, OWN, cy), BF16),
        vm((r, 2, 2, 4, OWN, cx), BF16),
        vm((r, 2, 2, 4, OWN, cy), BF16),
        vm((r, 2, 4, OWN, d_own), F32),
        vm((r, 2, 2, OWN, d_own), F32),
        vm((r, 2, 2, OWN, d_own), F32),
        vm((r, 2, 2, HALF, d_own), F32),
        vm((r, 2, 2, HALF, d_own), F32),
        vm((r, OWN, d_own), F32),
        vm((r, OWN, d_own), F32),
        vm((2, r, HALF, 128), F32),
        vm((4, 8, 128), F32),
        vm((4, 8, 128), F32),
        pltpu.SemaphoreType.DMA((5,)),
        pltpu.SemaphoreType.DMA((40, r)),
        pltpu.SemaphoreType.DMA((40, r)),
    ]
    held = pl.BlockSpec(memory_space=pltpu.VMEM)
    far = pl.BlockSpec(memory_space=pl.ANY)
    coeffs, offsets = pl.pallas_call(
        kernel,
        name="bound_pass",
        out_shape=(
            jax.ShapeDtypeStruct((spec_rows.shape[0] // 8, d_own), F32),
            jax.ShapeDtypeStruct((1, 64), F32),
        ),
        in_specs=[held, far, far, far, far, held, held, held, held, held],
        out_specs=(held, held),
        scratch_shapes=scratch,
        compiler_params=pltpu.CompilerParams(
            collective_id=0, has_side_effects=True, vmem_limit_bytes=60 * 1024 * 1024
        ),
    )(spec_rows, readout, gate_weight, up_weight, down_weight, *lanes)
    return coeffs, offsets.reshape(64)


def solution(mesh):
    placed = (
        P(),
        P(None, "wid"),
        P("wid", "hid"),
        P("wid", "hid"),
        P("hid", "wid"),
        P("hid"),
        P("hid"),
        P("hid"),
        P("hid"),
        P("hid"),
    )
    return jax.shard_map(
        per_device,
        mesh=mesh,
        in_specs=placed,
        out_specs=(P("hid", "wid"), P("wid")),
        check_vma=False,
    )
```

time: 388 us -> 117 us (0.30)
  waiting for transfers between devices: 301 us -> 0 us
  Pallas kernels: 0 us -> 112 us
  matrix products: 28.8 us -> 0 us
  blocking collectives: 25 us -> 0 us
  between operations: 13.9 us -> 0.64 us
  local copies, waits for them, and re-layouts: 12.2 us -> 4.46 us
  other arithmetic: 6.39 us -> 0 us
    reduce_scatter x2 -> x0, waiting for transfers between devices: 214 us -> none  [the longest x1 163 us: per_device(): lax.psum_scatter(lax.dot_general(lam, down_weight, dims, preferred_elemen...]
    pallas_call x0 -> x1, Pallas kernels: none -> 112 us  [per_device(): pl.pallas_call(kernel, name='bound_pass', out_shape=(jax.ShapeDtypeStruct...]
    all_gather x2 -> x0, waiting for transfers between devices: 85.8 us -> none  [the longest x1 45.3 us: per_device(): lax.all_gather(lam_g, 'wid', axis=0, tiled=True)]
    dot_general x3 -> x0, matrix products: 28.8 us -> none  [the longest x1 10.1 us: per_device(): lax.dot_general(lam_u, up_weight, dims, preferred_element_type=jnp.float32)]
    psum x1 -> x0, blocking collectives: 25 us -> none  [per_device(): offsets = lax.psum(partial_offsets, 'hid')]
    gather x2 -> x0, local copies, waits for them, and re-layouts: 9.03 us -> none  [the longest x1 5.08 us: per_device(): rival = jnp.take(readout, spec_rows[:, 1], axis=0).astype(jnp.float32)]
  transfers between devices with their start and end apart: 4 -> 0, of which waited for: 4 -> 0; matrix products, arithmetic and copies ran while one was open for 2% -> 0% of each run, Pallas kernels for 0% -> 0%
where the time goes in v1:
time: 117 us
  Pallas kernels  112 us (96%)
  local copies, waits for them, and re-layouts  4.46 us (4%)
    pallas_call x1, Pallas kernels, per_device(): pl.pallas_call(kernel, name='bound_pass', out_shape=(jax.ShapeDtypeStruct...  112 us
    unnamed x3, local copies, waits for them, and re-layouts  4.46 us

profile of v1, /device:TPU:0, one launch (start us, length us, event | category | flops | bytes accessed | tf_op | source)
XLA Modules:
  0.0 117.0 jit_solution(10654295849908840851)
XLA Ops:
  0.6 1.7 %copy.12.spec = s32[1024,2]{1,0:T(8,128)} copy(s32[1024,2]{0,1:T(2,128)} %param.10) | data formatting | bytes 16384 | tf_op args[0]
  2.3 111.9 %bound_pass.1 = (f32[128,512]{1,0:T(8,128)}, f32[1,64]{1,0:T(1,128)}) custom-call(s32[1024,2]{1,0:T(8,128)} %copy.12.spec, bf16[2048,512]{1,0:T(8,128)(2,1)} %readout.1, bf16[512,3584]{1,0:T(8,128)(2,1)} %gate.1, bf16[512,3584]{1,0:T(8,128)(2,1)} %up.1, bf16[3584,512]{1,0:T(8,128)(2,1)} %down.1, f32[28,128]{1,0:T(8,128)} %bitcast.6, f32[28,128]{1,0:T(8,128)} %bitcast.7, ...), custom_call_target="tpu_custom_call" | custom-call | tf_op jit(solution)/shard_map/bound_pass/pallas_call | solution.py:504
  114.2 1.7 %copy.15 = f32[128,512]{1,0:T(8,128)} copy(f32[128,512]{1,0:T(8,128)} %get-tuple-element.8) | data formatting | bytes 524288
  115.9 1.1 copy.16

commit v2 on v1

--- a/solution.py
+++ b/solution.py
@@ -1,5 +1,3 @@
-import functools
-
 import jax
 import jax.numpy as jnp
 from jax import lax
@@ -46,35 +44,26 @@
     return au, as_lower * slope, as_upper * slope, kp, kn
 
 
-STEPS = {
-    "lam": 0.0,
-    "down": 1.5,
-    "x1": 7.0,
-    "y1": 7.1,
-    "x2": 10.0,
-    "y2": 10.1,
-    "x3": 13.0,
-    "y3": 13.1,
-    "gx1": 16.0,
-    "gy1": 16.1,
-    "gx2": 19.0,
-    "gy2": 19.1,
-    "gx3": 22.0,
-    "gy3": 22.1,
-    "mm": 24.0,
-    "z1": 28.0,
-    "z2": 31.0,
-    "out": 34.0,
-}
-STARTS = (0.0, 4.0, 14.0, 25.0)
+PLAN = (
+    ("lam", 0), ("lam", 1), ("downx", 0), ("downy", 0), ("downx", 1), ("downy", 1), ("lam", 2), ("y1", 0),
+    ("x1", 0), ("downx", 2), ("y1", 1), ("downy", 2), ("y2", 0), ("x2", 0), ("x1", 1), ("x3", 0), ("y2", 1),
+    ("x2", 1), ("y3", 0), ("lam", 3), ("x1", 2), ("gx1", 0), ("y3", 1), ("gy1", 0), ("w", 0), ("x3", 1),
+    ("gx2", 0), ("downx", 3), ("x2", 2), ("gy1", 1), ("gy2", 0), ("gx3", 0), ("y1", 2), ("x3", 2), ("gy3", 0),
+    ("gx1", 1), ("gy2", 1), ("downy", 3), ("y2", 2), ("w", 1), ("x1", 3), ("gx2", 1), ("mma", 0), ("y3", 2),
+    ("gx1", 2), ("gy3", 1), ("mm", 0), ("gx3", 1), ("y1", 3), ("mma", 1), ("x2", 3), ("gy1", 2), ("y2", 3),
+    ("x3", 3), ("mm", 1), ("gx2", 2), ("gy2", 2), ("y3", 3), ("o", 0), ("gx3", 2), ("gx1", 3), ("o", 1),
+    ("gy3", 2), ("gy1", 3), ("mma", 2), ("mm", 2), ("z1", 1), ("gy3", 3), ("z1", 0), ("gx3", 3), ("o", 2),
+    ("mma", 3), ("mm", 3), ("o", 3), ("z1", 2), ("out", 0), ("out", 1), ("o", 4), ("out", 3), ("out", 2),
+)
+LAST = CHUNKS - 1
 
 
 def kernel(
     spec, readout, gate, up, down, gate_lo, gate_width, up_lo, up_width, flags,
     out, off,
-    ro, wp, wn, dn, ds, oh, lam, lams, tab,
+    ro, wp, wn, dn, pairs, oh, lam, tab,
     px, py, x1s, x1r, xps, xpr, xqs, xqr, yps, ypr, yqs, yqr, yxs, yxr,
-    lx, ly, acc, zps, zpr, zqs, zqr, hs, hr, oacc, obs, obr,
+    lx, ly, acc, zr, hs, hr, ends, endr, oacc, obs, obr,
     lsem, ssem, rsem,
 ):
     hid, wid = lax.axis_index("hid"), lax.axis_index("wid")
@@ -82,8 +71,9 @@
     y, a, c = wid // 4, (wid // 2) % 2, wid % 2
     half = dn.shape[0]
     cx, cy = px.shape[-1], py.shape[-1]
-    d_own = dn.shape[1]
-    rows = CHUNKS * 0 + 8 * OWN
+    d_own = ro.shape[1]
+    rows = 8 * OWN
+    mine, its = pl.ds(0, d_own), pl.ds(d_own, d_own)
     yu, yd, yo = (y + 1) % 4, (y + 3) % 4, (y + 2) % 4
     zu, zd, zo = (z + 1) % 4, (z + 3) % 4, (z + 2) % 4
 
@@ -93,20 +83,21 @@
     up_y, down_y = at(z, xh, yu, a, c), at(z, xh, yd, a, c)
     other_x = at(z, xh, y, 1 - a, c)
     twin = at(z, xh, y, a, 1 - c)
-    up_z, down_z = at(zu, xh, y, a, c), at(zd, xh, y, a, c)
-    other_h = at(z, 1 - xh, y, a, c)
+    over_y = at(z, xh, yo, a, c)
+    by_z = {(s, f): at((z + s) % 4, (xh + f) % 2, y, a, c) for s in range(4) for f in range(2) if s or f}
+    other_h = by_z[0, 1]
 
     barrier = pltpu.get_barrier_semaphore()
-    for device in (up_y, down_y, other_x, twin, up_z, down_z, other_h):
+    for device in (up_y, down_y, over_y, other_x, twin, *by_z.values()):
         pl.semaphore_signal(barrier, inc=1, device_id=device, device_id_type=MESH)
 
     load_ro = pltpu.make_async_copy(readout, ro, lsem.at[0])
     load_ro.start()
     my_half = pl.multiple_of(c * half, half)
     its_half = pl.multiple_of((1 - c) * half, half)
-    load_dx = pltpu.make_async_copy(down.at[pl.ds(my_half, cx)], dn.at[pl.ds(0, cx)], lsem.at[1])
+    load_dx = pltpu.make_async_copy(down.at[pl.ds(my_half, cx)], dn.at[pl.ds(0, cx), mine], lsem.at[1])
     load_dy = pltpu.make_async_copy(
-        down.at[pl.ds(pl.multiple_of(my_half + cx, 256), cy)], dn.at[pl.ds(cx, cy)], lsem.at[2]
+        down.at[pl.ds(pl.multiple_of(my_half + cx, 256), cy)], dn.at[pl.ds(cx, cy), mine], lsem.at[2]
     )
     load_dx.start()
     load_dy.start()
@@ -135,18 +126,22 @@
     ):
         tab[k, 0 : table.shape[0], :] = table
 
+    tall = jnp.concatenate([spec[...].astype(F32), jnp.zeros((6, spec.shape[1]), F32)], axis=0)
+    pairs[...] = tall.T
+    oacc[...] = jnp.zeros_like(oacc)
+
     def lam_rows(r):
         def group(g, carry):
             a_, y_, co = g // 8, (g // 2) % 4, g % 2
             start = pl.multiple_of((y_ * 2 + a_) * 128 + co * 64 + r * 16, 16)
-            pair = spec[pl.ds(start, 16), :]
+            pair = pairs[pl.ds(start, 16), :].astype(jnp.int32)
             classes = lax.broadcasted_iota(jnp.int32, (16, ro.shape[0]), 1)
             picked = jnp.where(classes == pair[:, 0:1], 1.0, 0.0) - jnp.where(classes == pair[:, 1:2], 1.0, 0.0)
             oh[pl.ds(pl.multiple_of(g * 16, 16), 16), :] = picked.astype(BF16)
             return carry
 
         lax.fori_loop(0, 16, group, 0)
-        lam[r] = jnp.dot(oh[...], ro[...], preferred_element_type=F32).astype(BF16)
+        lam[r, :, 0:d_own] = jnp.dot(oh[...], ro[...], preferred_element_type=F32).astype(BF16)
 
     def tree_first(stage, get, u, d, o):
         lead = (slice(None),) * (len(stage.shape) - 3)
@@ -186,60 +181,50 @@
             part = value[:, j * 128 : (j + 1) * 128]
             total = total + jnp.maximum(part, 0.0) * tab[3, pl.ds(row, 1), :]
             total = total + jnp.minimum(part, 0.0) * tab[4, pl.ds(row, 1), :]
-        if first == 0:
-            oacc[h, r] = total
-        else:
-            oacc[h, r] += total
+        oacc[h, r] += total
 
     def step_lam(r):
         if r == 0:
             load_ro.wait()
         lam_rows(r)
         if r == 0:
-            pl.semaphore_wait(barrier, 7)
-            send("lam", r, lam.at[r], lams.at[r], twin)
-            send("dx", 0, down.at[pl.ds(its_half, cx)], ds.at[pl.ds(0, cx)], twin)
-            send("dy", 0, down.at[pl.ds(pl.multiple_of(its_half + cx, 256), cy)], ds.at[pl.ds(cx, cy)], twin)
-        else:
-            send("lam", r, lam.at[r], lams.at[r], twin)
-
-    def times_down(r, first, count, target):
-        def block(n, carry):
-            units = pl.ds(pl.multiple_of(first + n * 256, 256), 256)
-            part = lax.dot_general(lam[r], dn[units, :], NT, preferred_element_type=F32)
-            part = part + lax.dot_general(lams[r], ds[units, :], NT, preferred_element_type=F32)
-            target(pl.ds(pl.multiple_of(n * 256, 256), 256), part)
-            return carry
-
-        lax.fori_loop(0, count // 256, block, 0)
-
-    def step_down(r):
-        arrive("lam", r)
+            pl.semaphore_wait(barrier, 5 + len(by_z))
+        send("lam", r, lam.at[r, :, mine], lam.at[r, :, its], twin)
+        if r == 0:
+            send("dx", 0, down.at[pl.ds(its_half, cx)], dn.at[pl.ds(0, cx), its], twin)
+            later = pl.ds(pl.multiple_of(its_half + cx, 256), cy)
+            send("dy", 0, down.at[later], dn.at[pl.ds(cx, cy), its], twin)
+
+    def times_down(r, units):
+        return lax.dot_general(lam[r], dn[units, :], NT, preferred_element_type=F32)
+
+    def step_downx(r):
         if r == 0:
             load_dx.wait()
             arrive("dx", 0)
-
-        def to_x(columns, part):
-            px[r, :, :, columns] = part.reshape(8, OWN, 256)
-
-        def to_y(columns, part):
-            py[r, :, :, :, columns] = part.reshape(2, 4, OWN, 256)
-
-        times_down(r, 0, cx, to_x)
+        arrive("lam", r)
+        for n in range(cx // 256):
+            columns = slice(n * 256, (n + 1) * 256)
+            px[r, :, :, columns] = times_down(r, columns).reshape(8, OWN, 256)
         x1s[r] = px[r, pl.ds((1 - a) * 4, 4)].astype(BF16)
         send("x1", r, x1s.at[r], x1r.at[r], other_x)
+
+    def step_downy(r):
         if r == 0:
             load_dy.wait()
             arrive("dy", 0)
-        times_down(r, cx, cy, to_y)
+        for n in range(cy // 256):
+            columns = slice(n * 256, (n + 1) * 256)
+            units = slice(cx + n * 256, cx + (n + 1) * 256)
+            py[r, :, :, :, columns] = times_down(r, units).reshape(2, 4, OWN, 256)
         tree_first(yps.at[r], get_y(r), yu, yd, yo)
         send("yu1", r, yps.at[r, 0], ypr.at[r, 0], up_y)
         send("yd1", r, yps.at[r, 1], ypr.at[r, 1], down_y)
 
     def step_x1(r):
         arrive("x1", r)
-        mine = pl.ds(a * 4, 4)
-        px[r, mine] += x1r[r].astype(F32)
+        own = pl.ds(a * 4, 4)
+        px[r, own] += x1r[r].astype(F32)
         tree_first(xps.at[r], get_x(r), yu, yd, yo)
         send("xu1", r, xps.at[r, 0], xpr.at[r, 0], up_y)
         send("xd1", r, xps.at[r, 1], xpr.at[r, 1], down_y)
@@ -277,6 +262,8 @@
         send("gxu1", r, block, block, up_y)
         send("gxd1", r, block, block, down_y)
         send("gxx0", r, block, block, other_x)
+        if r == LAST:
+            send("gxo", r, block, block, over_y)
 
     def step_y3(r):
         arrive("yx", r)
@@ -288,10 +275,20 @@
         send("gyx", r, block, block, other_x)
         send("gyu1", r, block, block, up_y)
         send("gyd1", r, block, block, down_y)
+        if r == LAST:
+            send("gyo", r, block, block, over_y)
 
     def step_gx1(r):
         arrive("gxu1", r)
         arrive("gxd1", r)
+        if r == LAST:
+            arrive("gxo", r)
+            for name, y_ in (("gxx1", yu), ("gxx2", yd), ("gxx3", yo)):
+                block = lx.at[r, c, a, y_]
+                send(name, r, block, block, other_x)
+            block = lx.at[r, c, a]
+            send("tx0", r, block, block, twin)
+            return
         below = lx.at[r, c, a, yd, halves(0)]
         above = lx.at[r, c, a, yu, halves(1)]
         send("gxu2", r, below, below, up_y)
@@ -305,6 +302,8 @@
         block = ly.at[r, c, 1 - a, y]
         send("gyu1b", r, block, block, up_y)
         send("gyd1b", r, block, block, down_y)
+        if r == LAST:
+            send("gyob", r, block, block, over_y)
 
     def step_gx2(r):
         arrive("gxu2", r)
@@ -329,8 +328,12 @@
         send("tx1", r, block, block, twin)
 
     def step_gy3(r):
-        arrive("gyu2", r)
-        arrive("gyd2", r)
+        if r == LAST:
+            for name in ("gyu1", "gyd1", "gyu1b", "gyd1b", "gyo", "gyob"):
+                arrive(name, r)
+        else:
+            arrive("gyu2", r)
+            arrive("gyd2", r)
         block = ly.at[r, c]
         send("ty", r, block, block, twin)
 
@@ -356,38 +359,41 @@
 
         lax.fori_loop(0, d_own // 256, block, 0)
 
+    def step_mma(r):
+        times_weights(r, c, False)
+
     def step_mm(r):
-        times_weights(r, c, False)
         arrive("tx0", r)
         arrive("tx1", r)
         arrive("ty", r)
         times_weights(r, 1 - c, True)
-        tree_first(zps.at[r], get_z(r), zu, zd, zo)
-        send("zu1", r, zps.at[r, 0], zpr.at[r, 0], up_z)
-        send("zd1", r, zps.at[r, 1], zpr.at[r, 1], down_z)
+        if r == LAST:
+            ends[...] = acc[r].astype(BF16)
+            for (s, f), device in by_z.items():
+                send("e%d%d" % (s, f), r, ends.at[(xh + f) % 2, (z + s) % 4], endr.at[s * 2 + f], device)
+        else:
+            for s, z_ in ((1, zu), (3, zd), (2, zo)):
+                send("z%d" % s, r, acc.at[r, :, z_], zr.at[r, s - 1], by_z[s, 0])
 
     def step_z1(r):
-        arrive("zu1", r)
-        arrive("zd1", r)
-        tree_second(zqs.at[r], zpr.at[r], get_z(r), zu, zd)
-        send("zu2", r, zqs.at[r, 0], zqr.at[r, 0], up_z)
-        send("zd2", r, zqs.at[r, 1], zqr.at[r, 1], down_z)
-
-    def step_z2(r):
-        arrive("zu2", r)
-        arrive("zd2", r)
-        low, high = tree_last(zpr.at[r], zqr.at[r], get_z(r), z)
-        acc[r, :, z, halves(0)] = low
-        acc[r, :, z, halves(1)] = high
-        hs[r] = acc[r, 1 - xh, z]
+        for s in (1, 3, 2):
+            arrive("z%d" % s, r)
+        hs[r] = (acc[r, 1 - xh, z] + zr[r, 0, 1 - xh]) + (zr[r, 1, 1 - xh] + zr[r, 2, 1 - xh])
         send("h", r, hs.at[r], hr.at[r], other_h)
 
     def step_out(r):
-        arrive("h", r)
-        first = (xh * 4 + z) * OWN
+        first = pl.multiple_of((xh * 4 + z) * OWN, OWN)
+        total = lam[r, pl.ds(first, OWN), 0:d_own].astype(F32) + acc[r, xh, z]
+        if r == LAST:
+            for s, f in by_z:
+                arrive("e%d%d" % (s, f), r)
+                total = total + endr[s * 2 + f].astype(F32)
+        else:
+            total = total + (zr[r, 0, xh] + zr[r, 1, xh] + zr[r, 2, xh])
+            arrive("h", r)
+            total = total + hr[r]
         for h in range(2):
-            own = lam[r, pl.ds(pl.multiple_of(first + h * HALF, HALF), HALF), :].astype(F32)
-            out[h * 64 + r * HALF : h * 64 + (r + 1) * HALF, :] = own + acc[r, xh, z, halves(h)] + hr[r, halves(h)]
+            out[h * 64 + r * HALF : h * 64 + (r + 1) * HALF, :] = total[halves(h)]
 
     def weights(k):
         if k == 0:
@@ -417,6 +423,9 @@
         send("o", 0, obs.at[0], obr.at[0], partners[0])
 
     def offset_step(k):
+        if k == 0:
+            offset_start()
+            return
         arrive("o", k - 1)
         if k < 4:
             obs[k] = obs[k - 1] + obr[k - 1]
@@ -426,23 +435,12 @@
             off[...] = jnp.where(c == 0, total[0:1, 0:64], total[0:1, 64:128])
 
     table = dict(
-        lam=step_lam, down=step_down, x1=step_x1, y1=step_y1, x2=step_x2, y2=step_y2, x3=step_x3, y3=step_y3,
-        gx1=step_gx1, gy1=step_gy1, gx2=step_gx2, gy2=step_gy2, gx3=step_gx3, gy3=step_gy3,
-        mm=step_mm, z1=step_z1, z2=step_z2, out=step_out,
+        lam=step_lam, downx=step_downx, downy=step_downy, x1=step_x1, y1=step_y1, x2=step_x2, y2=step_y2,
+        x3=step_x3, y3=step_y3, gx1=step_gx1, gy1=step_gy1, gx2=step_gx2, gy2=step_gy2, gx3=step_gx3, gy3=step_gy3,
+        mma=step_mma, mm=step_mm, z1=step_z1, out=step_out, w=weights, o=offset_step,
     )
-    plan = [
-        (start + when, functools.partial(table[name], r))
-        for r, start in enumerate(STARTS)
-        for name, when in STEPS.items()
-    ]
-    plan.append((STARTS[1] + 2.0, functools.partial(weights, 0)))
-    plan.append((STARTS[1] + 6.05, functools.partial(weights, 1)))
-    last = STARTS[-1]
-    plan.append((last + 13.2, offset_start))
-    for k, when in ((1, 19.2), (2, 22.2), (3, 28.2), (4, 31.2)):
-        plan.append((last + when, functools.partial(offset_step, k)))
-    for _, step in sorted(plan, key=lambda item: item[0]):
-        step()
+    for name, r in PLAN:
+        table[name](r)
     for copy in copies.values():
         copy.wait_send()
 
@@ -463,11 +461,10 @@
         vm((readout.shape[0], d_own), BF16),
         vm((d_own, units), BF16),
         vm((d_own, units), BF16),
-        vm((half, d_own), BF16),
-        vm((half, d_own), BF16),
+        vm((half, 2 * d_own), BF16),
+        vm((spec_rows.shape[0], 8), F32),
         vm((rows, readout.shape[0]), BF16),
-        vm((r, rows, d_own), BF16),
-        vm((r, rows, d_own), BF16),
+        vm((r, rows, 2 * d_own), BF16),
         vm((5, 32, 128), F32),
         vm((r, 8, OWN, cx), F32),
         vm((r, 2, 4, OWN, cy), F32),
@@ -486,18 +483,17 @@
         vm((r, 2, 2, 4, OWN, cx), BF16),
         vm((r, 2, 2, 4, OWN, cy), BF16),
         vm((r, 2, 4, OWN, d_own), F32),
-        vm((r, 2, 2, OWN, d_own), F32),
-        vm((r, 2, 2, OWN, d_own), F32),
-        vm((r, 2, 2, HALF, d_own), F32),
-        vm((r, 2, 2, HALF, d_own), F32),
+        vm((r, 3, 2, OWN, d_own), F32),
         vm((r, OWN, d_own), F32),
         vm((r, OWN, d_own), F32),
+        vm((2, 4, OWN, d_own), BF16),
+        vm((8, OWN, d_own), BF16),
         vm((2, r, HALF, 128), F32),
         vm((4, 8, 128), F32),
         vm((4, 8, 128), F32),
         pltpu.SemaphoreType.DMA((5,)),
-        pltpu.SemaphoreType.DMA((40, r)),
-        pltpu.SemaphoreType.DMA((40, r)),
+        pltpu.SemaphoreType.DMA((48, r)),
+        pltpu.SemaphoreType.DMA((48, r)),
     ]
     held = pl.BlockSpec(memory_space=pltpu.VMEM)
     far = pl.BlockSpec(memory_space=pl.ANY)
@@ -514,7 +510,7 @@
         compiler_params=pltpu.CompilerParams(
             collective_id=0, has_side_effects=True, vmem_limit_bytes=60 * 1024 * 1024
         ),
-    )(spec_rows, readout, gate_weight, up_weight, down_weight, *lanes)
+    )(spec_rows.T, readout, gate_weight, up_weight, down_weight, *lanes)
     return coeffs, offsets.reshape(64)
 
 

time: 117 us -> 90.4 us (0.77)
  Pallas kernels: 112 us -> 86.7 us
  local copies, waits for them, and re-layouts: 4.46 us -> 2.8 us
    pallas_call x1, Pallas kernels: 112 us -> 86.7 us  [per_device(): pl.pallas_call(kernel, name='bound_pass', out_shape=(jax.ShapeDtypeStruct...]
    unnamed x3 -> x2, local copies, waits for them, and re-layouts: 4.46 us -> 2.8 us
where the time goes in v2:
time: 90.4 us; the launch traced here: 90.1 us
  Pallas kernels  86.7 us (96%)
  local copies, waits for them, and re-layouts  2.8 us (3%)
    pallas_call x1, Pallas kernels, per_device(): pl.pallas_call(kernel, name='bound_pass', out_shape=(jax.ShapeDtypeStruct...  86.7 us
    unnamed x2, local copies, waits for them, and re-layouts  2.8 us

profile of v2, /device:TPU:0, one launch (start us, length us, event | category | flops | bytes accessed | tf_op | source)
XLA Modules:
  0.0 90.1 jit_solution(10359945005759068784)
XLA Ops:
  0.6 86.7 %bound_pass.1 = (f32[128,512]{1,0:T(8,128)}, f32[1,64]{1,0:T(1,128)}) custom-call(s32[2,1024]{1,0:T(2,128)} %bitcast.12, bf16[2048,512]{1,0:T(8,128)(2,1)} %readout.1, bf16[512,3584]{1,0:T(8,128)(2,1)} %gate.1, bf16[512,3584]{1,0:T(8,128)(2,1)} %up.1, bf16[3584,512]{1,0:T(8,128)(2,1)} %down.1, f32[28,128]{1,0:T(8,128)} %bitcast.7, f32[28,128]{1,0:T(8,128)} %bitcast.8, ...), custom_call_target="tpu_custom_call" | custom-call | tf_op jit(solution)/shard_map/bound_pass/pallas_call | solution.py:500
  87.3 1.7 %copy.14 = f32[128,512]{1,0:T(8,128)} copy(f32[128,512]{1,0:T(8,128)} %get-tuple-element.8) | data formatting | bytes 524288
  89.0 1.1 %copy.15 = f32[64]{0:T(128)} copy(f32[64]{0:T(128)} %bitcast.13) | data formatting | bytes 512

commit v3 on v2

--- a/solution.py
+++ b/solution.py
@@ -45,17 +45,18 @@
 
 
 PLAN = (
-    ("lam", 0), ("lam", 1), ("downx", 0), ("downy", 0), ("downx", 1), ("downy", 1), ("lam", 2), ("y1", 0),
-    ("x1", 0), ("downx", 2), ("y1", 1), ("downy", 2), ("y2", 0), ("x2", 0), ("x1", 1), ("x3", 0), ("y2", 1),
-    ("x2", 1), ("y3", 0), ("lam", 3), ("x1", 2), ("gx1", 0), ("y3", 1), ("gy1", 0), ("w", 0), ("x3", 1),
-    ("gx2", 0), ("downx", 3), ("x2", 2), ("gy1", 1), ("gy2", 0), ("gx3", 0), ("y1", 2), ("x3", 2), ("gy3", 0),
-    ("gx1", 1), ("gy2", 1), ("downy", 3), ("y2", 2), ("w", 1), ("x1", 3), ("gx2", 1), ("mma", 0), ("y3", 2),
-    ("gx1", 2), ("gy3", 1), ("mm", 0), ("gx3", 1), ("y1", 3), ("mma", 1), ("x2", 3), ("gy1", 2), ("y2", 3),
-    ("x3", 3), ("mm", 1), ("gx2", 2), ("gy2", 2), ("y3", 3), ("o", 0), ("gx3", 2), ("gx1", 3), ("o", 1),
-    ("gy3", 2), ("gy1", 3), ("mma", 2), ("mm", 2), ("z1", 1), ("gy3", 3), ("z1", 0), ("gx3", 3), ("o", 2),
-    ("mma", 3), ("mm", 3), ("o", 3), ("z1", 2), ("out", 0), ("out", 1), ("o", 4), ("out", 3), ("out", 2),
+    ("lam", 0), ("lam", 1), ("downx", 0), ("downy", 0), ("lam", 2), ("downx", 1), ("downy", 1), ("y1", 0),
+    ("lam", 3), ("x1", 0), ("downx", 2), ("y1", 1), ("y2", 0), ("x1", 1), ("x2", 0), ("downy", 2), ("y2", 1),
+    ("downx", 3), ("x2", 1), ("x3", 0), ("y3", 0), ("x1", 2), ("y3", 1), ("y1", 2), ("x3", 1), ("downy", 3),
+    ("gy1", 0), ("gx1", 0), ("gy1", 1), ("w", 0), ("gx2", 0), ("x2", 2), ("y2", 2), ("x1", 3), ("gy2", 0),
+    ("gx1", 1), ("y1", 3), ("gx3", 0), ("y3", 2), ("w", 1), ("x3", 2), ("gx2", 1), ("x2", 3), ("gy3", 0),
+    ("mma", 0), ("gy2", 1), ("y2", 3), ("gy1", 2), ("mm", 0), ("x3", 3), ("gx1", 2), ("gy3", 1), ("y3", 3),
+    ("o", 0), ("gx3", 1), ("gy2", 2), ("mma", 1), ("gx2", 2), ("mm", 1), ("gx1", 3), ("o", 1), ("gy1", 3),
+    ("gx3", 2), ("gy3", 2), ("z1", 0), ("mma", 2), ("mm", 2), ("gx3", 3), ("gy3", 3), ("o", 2), ("mma", 3),
+    ("z1", 1), ("mm", 3), ("o", 3), ("out", 0), ("out", 2), ("out", 1), ("o", 4), ("out", 3),
 )
-LAST = CHUNKS - 1
+STRAIGHT = (2, 3)
+SPREAD = (3,)
 
 
 def kernel(
@@ -103,20 +104,21 @@
     load_dy.start()
     load_up = pltpu.make_async_copy(up, wp, lsem.at[3])
     load_gate = pltpu.make_async_copy(gate, wn, lsem.at[4])
-    load_up.start()
-    load_gate.start()
 
     copies = {}
+    unsent = {}
     index = {}
 
     def send(name, r, src, dst, device):
-        k = index.setdefault(name, len(index))
+        if (name, r - 2) in unsent:
+            unsent.pop((name, r - 2)).wait_send()
+        k = index.setdefault((name, r % 2), len(index))
         copy = pltpu.make_async_remote_copy(
-            src_ref=src, dst_ref=dst, send_sem=ssem.at[k, r], recv_sem=rsem.at[k, r],
+            src_ref=src, dst_ref=dst, send_sem=ssem.at[k], recv_sem=rsem.at[len(copies)],
             device_id=device, device_id_type=MESH,
         )
         copy.start()
-        copies[name, r] = copy
+        copies[name, r] = unsent[name, r] = copy
 
     def arrive(name, r):
         copies[name, r].wait_recv()
@@ -130,7 +132,7 @@
     pairs[...] = tall.T
     oacc[...] = jnp.zeros_like(oacc)
 
-    def lam_rows(r):
+    def pick_rows(r):
         def group(g, carry):
             a_, y_, co = g // 8, (g // 2) % 4, g % 2
             start = pl.multiple_of((y_ * 2 + a_) * 128 + co * 64 + r * 16, 16)
@@ -141,6 +143,8 @@
             return carry
 
         lax.fori_loop(0, 16, group, 0)
+
+    def lam_rows(r):
         lam[r, :, 0:d_own] = jnp.dot(oh[...], ro[...], preferred_element_type=F32).astype(BF16)
 
     def tree_first(stage, get, u, d, o):
@@ -184,16 +188,15 @@
         oacc[h, r] += total
 
     def step_lam(r):
-        if r == 0:
-            load_ro.wait()
-        lam_rows(r)
+        pick_rows(r)
         if r == 0:
             pl.semaphore_wait(barrier, 5 + len(by_z))
-        send("lam", r, lam.at[r, :, mine], lam.at[r, :, its], twin)
-        if r == 0:
             send("dx", 0, down.at[pl.ds(its_half, cx)], dn.at[pl.ds(0, cx), its], twin)
             later = pl.ds(pl.multiple_of(its_half + cx, 256), cy)
             send("dy", 0, down.at[later], dn.at[pl.ds(cx, cy), its], twin)
+            load_ro.wait()
+        lam_rows(r)
+        send("lam", r, lam.at[r, :, mine], lam.at[r, :, its], twin)
 
     def times_down(r, units):
         return lax.dot_general(lam[r], dn[units, :], NT, preferred_element_type=F32)
@@ -211,6 +214,8 @@
 
     def step_downy(r):
         if r == 0:
+            load_up.start()
+            load_gate.start()
             load_dy.wait()
             arrive("dy", 0)
         for n in range(cy // 256):
@@ -262,7 +267,7 @@
         send("gxu1", r, block, block, up_y)
         send("gxd1", r, block, block, down_y)
         send("gxx0", r, block, block, other_x)
-        if r == LAST:
+        if r in SPREAD:
             send("gxo", r, block, block, over_y)
 
     def step_y3(r):
@@ -275,13 +280,13 @@
         send("gyx", r, block, block, other_x)
         send("gyu1", r, block, block, up_y)
         send("gyd1", r, block, block, down_y)
-        if r == LAST:
+        if r in SPREAD:
             send("gyo", r, block, block, over_y)
 
     def step_gx1(r):
         arrive("gxu1", r)
         arrive("gxd1", r)
-        if r == LAST:
+        if r in SPREAD:
             arrive("gxo", r)
             for name, y_ in (("gxx1", yu), ("gxx2", yd), ("gxx3", yo)):
                 block = lx.at[r, c, a, y_]
@@ -302,7 +307,7 @@
         block = ly.at[r, c, 1 - a, y]
         send("gyu1b", r, block, block, up_y)
         send("gyd1b", r, block, block, down_y)
-        if r == LAST:
+        if r in SPREAD:
             send("gyob", r, block, block, over_y)
 
     def step_gx2(r):
@@ -328,7 +333,7 @@
         send("tx1", r, block, block, twin)
 
     def step_gy3(r):
-        if r == LAST:
+        if r in SPREAD:
             for name in ("gyu1", "gyd1", "gyu1b", "gyd1b", "gyo", "gyob"):
                 arrive(name, r)
         else:
@@ -357,7 +362,7 @@
                 acc[r, :, :, :, units] = total
             return carry
 
-        lax.fori_loop(0, d_own // 256, block, 0)
+        lax.fori_loop(0, d_own // 256, block, 0, unroll=True)
 
     def step_mma(r):
         times_weights(r, c, False)
@@ -367,10 +372,11 @@
         arrive("tx1", r)
         arrive("ty", r)
         times_weights(r, 1 - c, True)
-        if r == LAST:
-            ends[...] = acc[r].astype(BF16)
+        if r in STRAIGHT:
+            k = STRAIGHT.index(r)
+            ends[k] = acc[r].astype(BF16)
             for (s, f), device in by_z.items():
-                send("e%d%d" % (s, f), r, ends.at[(xh + f) % 2, (z + s) % 4], endr.at[s * 2 + f], device)
+                send("e%d%d" % (s, f), r, ends.at[k, (xh + f) % 2, (z + s) % 4], endr.at[k, s * 2 + f], device)
         else:
             for s, z_ in ((1, zu), (3, zd), (2, zo)):
                 send("z%d" % s, r, acc.at[r, :, z_], zr.at[r, s - 1], by_z[s, 0])
@@ -381,13 +387,19 @@
         hs[r] = (acc[r, 1 - xh, z] + zr[r, 0, 1 - xh]) + (zr[r, 1, 1 - xh] + zr[r, 2, 1 - xh])
         send("h", r, hs.at[r], hr.at[r], other_h)
 
+    def drain(keys):
+        for key in keys:
+            unsent.pop(key).wait_send()
+
     def step_out(r):
+        if r == CHUNKS - 1:
+            drain(tuple(key for key in unsent if key[0][0] not in "hez"))
         first = pl.multiple_of((xh * 4 + z) * OWN, OWN)
         total = lam[r, pl.ds(first, OWN), 0:d_own].astype(F32) + acc[r, xh, z]
-        if r == LAST:
+        if r in STRAIGHT:
             for s, f in by_z:
                 arrive("e%d%d" % (s, f), r)
-                total = total + endr[s * 2 + f].astype(F32)
+                total = total + endr[STRAIGHT.index(r), s * 2 + f].astype(F32)
         else:
             total = total + (zr[r, 0, xh] + zr[r, 1, xh] + zr[r, 2, xh])
             arrive("h", r)
@@ -441,8 +453,12 @@
     )
     for name, r in PLAN:
         table[name](r)
-    for copy in copies.values():
-        copy.wait_send()
+    drain(tuple(unsent))
+
+
+def hand_over(coeffs, offsets, out, off):
+    out[...] = coeffs[...]
+    off[...] = offsets[...]
 
 
 def per_device(
@@ -486,14 +502,14 @@
         vm((r, 3, 2, OWN, d_own), F32),
         vm((r, OWN, d_own), F32),
         vm((r, OWN, d_own), F32),
-        vm((2, 4, OWN, d_own), BF16),
-        vm((8, OWN, d_own), BF16),
+        vm((len(STRAIGHT), 2, 4, OWN, d_own), BF16),
+        vm((len(STRAIGHT), 8, OWN, d_own), BF16),
         vm((2, r, HALF, 128), F32),
         vm((4, 8, 128), F32),
         vm((4, 8, 128), F32),
         pltpu.SemaphoreType.DMA((5,)),
-        pltpu.SemaphoreType.DMA((48, r)),
-        pltpu.SemaphoreType.DMA((48, r)),
+        pltpu.SemaphoreType.DMA((96,)),
+        pltpu.SemaphoreType.DMA((160,)),
     ]
     held = pl.BlockSpec(memory_space=pltpu.VMEM)
     far = pl.BlockSpec(memory_space=pl.ANY)
@@ -511,6 +527,13 @@
             collective_id=0, has_side_effects=True, vmem_limit_bytes=60 * 1024 * 1024
         ),
     )(spec_rows.T, readout, gate_weight, up_weight, down_weight, *lanes)
+    coeffs, offsets = pl.pallas_call(
+        hand_over,
+        name="hand_over",
+        out_shape=(jax.ShapeDtypeStruct(coeffs.shape, F32), jax.ShapeDtypeStruct(offsets.shape, F32)),
+        in_specs=[held, held],
+        out_specs=(held, held),
+    )(coeffs, offsets)
     return coeffs, offsets.reshape(64)
 
 

time: 90.4 us -> 84.8 us (0.938); the launches traced: 90.1 us -> 83.4 us
  Pallas kernels: 86.7 us -> 82.8 us
  local copies, waits for them, and re-layouts: 2.8 us -> 0 us
    pallas_call x1, Pallas kernels: 86.7 us -> 81.1 us  [per_device(): pl.pallas_call(kernel, name='bound_pass', out_shape=(jax.ShapeDtypeStruct...]
    unnamed x2 -> x0, local copies, waits for them, and re-layouts: 2.8 us -> none
    pallas_call x0 -> x1, Pallas kernels: none -> 1.68 us  [per_device(): pl.pallas_call(hand_over, name='hand_over', out_shape=(jax.ShapeDtypeStru...]
where the time goes in v3:
time: 84.8 us; the launch traced here: 83.4 us
  Pallas kernels  82.8 us (98%)
    pallas_call x1, Pallas kernels, per_device(): pl.pallas_call(kernel, name='bound_pass', out_shape=(jax.ShapeDtypeStruct...  81.1 us

profile of v3, /device:TPU:0, one launch (start us, length us, event | category | flops | bytes accessed | tf_op | source)
XLA Modules:
  0.0 83.4 jit_solution(8981030345332630617)
XLA Ops:
  0.6 81.1 %bound_pass.1 = (f32[128,512]{1,0:T(8,128)}, f32[1,64]{1,0:T(1,128)}) custom-call(s32[2,1024]{1,0:T(2,128)} %bitcast.12, bf16[2048,512]{1,0:T(8,128)(2,1)} %readout.1, bf16[512,3584]{1,0:T(8,128)(2,1)} %gate.1, bf16[512,3584]{1,0:T(8,128)(2,1)} %up.1, bf16[3584,512]{1,0:T(8,128)(2,1)} %down.1, f32[28,128]{1,0:T(8,128)} %bitcast.7, f32[28,128]{1,0:T(8,128)} %bitcast.8, ...), custom_call_target="tpu_custom_call" | custom-call | tf_op jit(solution)/shard_map/bound_pass/pallas_call | solution.py:516
  81.8 1.7 %hand_over.1 = (f32[128,512]{1,0:T(8,128)}, f32[1,64]{1,0:T(1,128)}) custom-call(f32[128,512]{1,0:T(8,128)} %get-tuple-element.6.coeffs, f32[1,64]{1,0:T(1,128)} %get-tuple-element.7.offsets), custom_call_target="tpu_custom_call" | custom-call | tf_op jit(solution)/shard_map/hand_over/pallas_call | solution.py:530

commit v4 on v3

--- a/solution.py
+++ b/solution.py
@@ -45,24 +45,24 @@
 
 
 PLAN = (
-    ("lam", 0), ("lam", 1), ("downx", 0), ("downy", 0), ("lam", 2), ("downx", 1), ("downy", 1), ("y1", 0),
-    ("lam", 3), ("x1", 0), ("downx", 2), ("y1", 1), ("y2", 0), ("x1", 1), ("x2", 0), ("downy", 2), ("y2", 1),
-    ("downx", 3), ("x2", 1), ("x3", 0), ("y3", 0), ("x1", 2), ("y3", 1), ("y1", 2), ("x3", 1), ("downy", 3),
-    ("gy1", 0), ("gx1", 0), ("gy1", 1), ("w", 0), ("gx2", 0), ("x2", 2), ("y2", 2), ("x1", 3), ("gy2", 0),
-    ("gx1", 1), ("y1", 3), ("gx3", 0), ("y3", 2), ("w", 1), ("x3", 2), ("gx2", 1), ("x2", 3), ("gy3", 0),
-    ("mma", 0), ("gy2", 1), ("y2", 3), ("gy1", 2), ("mm", 0), ("x3", 3), ("gx1", 2), ("gy3", 1), ("y3", 3),
-    ("o", 0), ("gx3", 1), ("gy2", 2), ("mma", 1), ("gx2", 2), ("mm", 1), ("gx1", 3), ("o", 1), ("gy1", 3),
-    ("gx3", 2), ("gy3", 2), ("z1", 0), ("mma", 2), ("mm", 2), ("gx3", 3), ("gy3", 3), ("o", 2), ("mma", 3),
-    ("z1", 1), ("mm", 3), ("o", 3), ("out", 0), ("out", 2), ("out", 1), ("o", 4), ("out", 3),
+    ("lam", 0), ("lam", 1), ("downx", 0), ("downy", 0), ("lam", 2), ("downx", 1), ("downy", 1), ("lam", 3),
+    ("y1", 0), ("downx", 2), ("x1", 0), ("downy", 2), ("y1", 1), ("downx", 3), ("y2", 0), ("x2", 0), ("downy", 3),
+    ("x1", 1), ("x3", 0), ("x2", 1), ("x1", 2), ("y2", 1), ("y1", 2), ("y3", 0), ("w", 0), ("gx1", 0), ("x3", 1),
+    ("x1", 3), ("y1", 3), ("x2", 2), ("y3", 1), ("gx2", 0), ("y2", 2), ("gy1", 0), ("gx1", 1), ("gy1", 1),
+    ("gx3", 0), ("x3", 2), ("y2", 3), ("gy2", 0), ("w", 1), ("x2", 3), ("gx2", 1), ("y3", 2), ("gy2", 1),
+    ("gy3", 0), ("x3", 3), ("y3", 3), ("o", 0), ("mma", 0), ("mm", 0), ("gy1", 2), ("gx1", 2), ("gx3", 1),
+    ("gy3", 1), ("mma", 1), ("gx1", 3), ("o", 1), ("gy1", 3), ("gx2", 2), ("gy2", 2), ("mm", 1), ("gx2", 3),
+    ("gy2", 3), ("gx3", 2), ("gy3", 2), ("z1", 0), ("mma", 2), ("gx3", 3), ("gy3", 3), ("o", 2), ("mm", 2),
+    ("mma", 3), ("mm", 3), ("o", 3), ("z1", 1), ("out", 0), ("out", 1), ("out", 2), ("o", 4), ("out", 3),
 )
 STRAIGHT = (2, 3)
-SPREAD = (3,)
+SPREAD = ()
 
 
 def kernel(
     spec, readout, gate, up, down, gate_lo, gate_width, up_lo, up_width, flags,
     out, off,
-    ro, wp, wn, dn, pairs, oh, lam, tab,
+    ro, wp, wn, dn, dt, pairs, oh, lam, tab,
     px, py, x1s, x1r, xps, xpr, xqs, xqr, yps, ypr, yqs, yqr, yxs, yxr,
     lx, ly, acc, zr, hs, hr, ends, endr, oacc, obs, obr,
     lsem, ssem, rsem,
@@ -100,7 +100,13 @@
     load_dy = pltpu.make_async_copy(
         down.at[pl.ds(pl.multiple_of(my_half + cx, 256), cy)], dn.at[pl.ds(cx, cy), mine], lsem.at[2]
     )
+    load_tx = pltpu.make_async_copy(down.at[pl.ds(its_half, cx)], dt.at[pl.ds(0, cx)], lsem.at[5])
+    load_ty = pltpu.make_async_copy(
+        down.at[pl.ds(pl.multiple_of(its_half + cx, 256), cy)], dt.at[pl.ds(cx, cy)], lsem.at[6]
+    )
+    load_tx.start()
     load_dx.start()
+    load_ty.start()
     load_dy.start()
     load_up = pltpu.make_async_copy(up, wp, lsem.at[3])
     load_gate = pltpu.make_async_copy(gate, wn, lsem.at[4])
@@ -191,12 +197,14 @@
         pick_rows(r)
         if r == 0:
             pl.semaphore_wait(barrier, 5 + len(by_z))
-            send("dx", 0, down.at[pl.ds(its_half, cx)], dn.at[pl.ds(0, cx), its], twin)
-            later = pl.ds(pl.multiple_of(its_half + cx, 256), cy)
-            send("dy", 0, down.at[later], dn.at[pl.ds(cx, cy), its], twin)
+            load_tx.wait()
+            send("dx", 0, dt.at[pl.ds(0, cx)], dn.at[pl.ds(0, cx), its], twin)
             load_ro.wait()
         lam_rows(r)
         send("lam", r, lam.at[r, :, mine], lam.at[r, :, its], twin)
+        if r == 0:
+            load_ty.wait()
+            send("dy", 0, dt.at[pl.ds(cx, cy)], dn.at[pl.ds(cx, cy), its], twin)
 
     def times_down(r, units):
         return lax.dot_general(lam[r], dn[units, :], NT, preferred_element_type=F32)
@@ -304,6 +312,8 @@
 
     def step_gy1(r):
         arrive("gyx", r)
+        block = ly.at[r, c, :, y]
+        send("ty0", r, block, block, twin)
         block = ly.at[r, c, 1 - a, y]
         send("gyu1b", r, block, block, up_y)
         send("gyd1b", r, block, block, down_y)
@@ -325,6 +335,9 @@
         above = ly.at[r, c, :, yu, halves(1)]
         send("gyu2", r, below, below, up_y)
         send("gyd2", r, above, above, down_y)
+        for name, y_ in (("ty1", yu), ("ty2", yd)):
+            block = ly.at[r, c, :, y_]
+            send(name, r, block, block, twin)
 
     def step_gx3(r):
         for k in range(4):
@@ -339,10 +352,11 @@
         else:
             arrive("gyu2", r)
             arrive("gyd2", r)
-        block = ly.at[r, c]
-        send("ty", r, block, block, twin)
-
-    def times_weights(r, cc, add):
+        for name, y_ in (("ty1", yu), ("ty2", yd), ("ty3", yo)) if r in SPREAD else (("ty3", yo),):
+            block = ly.at[r, c, :, y_]
+            send(name, r, block, block, twin)
+
+    def times_weights(r, cc, kinds, add):
         base = cc * half
         columns_x = pl.ds(pl.multiple_of(base, 256), cx)
         columns_y = pl.ds(pl.multiple_of(base + cx, 256), cy)
@@ -350,7 +364,7 @@
         def block(n, carry):
             units = pl.ds(pl.multiple_of(n * 256, 256), 256)
             total = None
-            for ref, columns in ((lx, columns_x), (ly, columns_y)):
+            for ref, columns in ((lx, columns_x), (ly, columns_y))[kinds]:
                 value = ref[r, cc].reshape(rows, columns.size)
                 for part, weight in ((jnp.maximum(value, 0), wp), (jnp.minimum(value, 0), wn)):
                     term = lax.dot_general(part, weight[units, columns], NT, preferred_element_type=F32)
@@ -365,13 +379,15 @@
         lax.fori_loop(0, d_own // 256, block, 0, unroll=True)
 
     def step_mma(r):
-        times_weights(r, c, False)
+        times_weights(r, c, slice(0, 2), False)
 
     def step_mm(r):
         arrive("tx0", r)
         arrive("tx1", r)
-        arrive("ty", r)
-        times_weights(r, 1 - c, True)
+        times_weights(r, 1 - c, slice(0, 1), True)
+        for k in range(4):
+            arrive("ty%d" % k, r)
+        times_weights(r, 1 - c, slice(1, 2), True)
         if r in STRAIGHT:
             k = STRAIGHT.index(r)
             ends[k] = acc[r].astype(BF16)
@@ -478,6 +494,7 @@
         vm((d_own, units), BF16),
         vm((d_own, units), BF16),
         vm((half, 2 * d_own), BF16),
+        vm((half, d_own), BF16),
         vm((spec_rows.shape[0], 8), F32),
         vm((rows, readout.shape[0]), BF16),
         vm((r, rows, 2 * d_own), BF16),
@@ -507,9 +524,9 @@
         vm((2, r, HALF, 128), F32),
         vm((4, 8, 128), F32),
         vm((4, 8, 128), F32),
-        pltpu.SemaphoreType.DMA((5,)),
-        pltpu.SemaphoreType.DMA((96,)),
-        pltpu.SemaphoreType.DMA((160,)),
+        pltpu.SemaphoreType.DMA((7,)),
+        pltpu.SemaphoreType.DMA((104,)),
+        pltpu.SemaphoreType.DMA((172,)),
     ]
     held = pl.BlockSpec(memory_space=pltpu.VMEM)
     far = pl.BlockSpec(memory_space=pl.ANY)

time: 84.8 us -> 83.4 us (0.983)
  no operation moved by 1% of the time
where the time goes in v4:
time: 83.4 us; the launch traced here: 82.8 us
  Pallas kernels  82.1 us (98%)
    pallas_call x1, Pallas kernels, per_device(): pl.pallas_call(kernel, name='bound_pass', out_shape=(jax.ShapeDtypeStruct...  80.5 us
    pallas_call x1, Pallas kernels, per_device(): pl.pallas_call(hand_over, name='hand_over', out_shape=(jax.ShapeDtypeStru...  1.68 us

profile of v4, /device:TPU:0, one launch (start us, length us, event | category | flops | bytes accessed | tf_op | source)
XLA Modules:
  0.0 82.8 jit_solution(11477812422467389311)
XLA Ops:
  0.6 80.5 %bound_pass.1 = (f32[128,512]{1,0:T(8,128)}, f32[1,64]{1,0:T(1,128)}) custom-call(s32[2,1024]{1,0:T(2,128)} %bitcast.12, bf16[2048,512]{1,0:T(8,128)(2,1)} %readout.1, bf16[512,3584]{1,0:T(8,128)(2,1)} %gate.1, bf16[512,3584]{1,0:T(8,128)(2,1)} %up.1, bf16[3584,512]{1,0:T(8,128)(2,1)} %down.1, f32[28,128]{1,0:T(8,128)} %bitcast.7, f32[28,128]{1,0:T(8,128)} %bitcast.8, ...), custom_call_target="tpu_custom_call" | custom-call | tf_op jit(solution)/shard_map/bound_pass/pallas_call | solution.py:533
  81.1 1.7 %hand_over.1 = (f32[128,512]{1,0:T(8,128)}, f32[1,64]{1,0:T(1,128)}) custom-call(f32[128,512]{1,0:T(8,128)} %get-tuple-element.6.coeffs, f32[1,64]{1,0:T(1,128)} %get-tuple-element.7.offsets), custom_call_target="tpu_custom_call" | custom-call | tf_op jit(solution)/shard_map/hand_over/pallas_call | solution.py:547

commit v5 on v4

--- a/solution.py
+++ b/solution.py
@@ -45,18 +45,18 @@
 
 
 PLAN = (
-    ("lam", 0), ("lam", 1), ("downx", 0), ("downy", 0), ("lam", 2), ("downx", 1), ("downy", 1), ("lam", 3),
-    ("y1", 0), ("downx", 2), ("x1", 0), ("downy", 2), ("y1", 1), ("downx", 3), ("y2", 0), ("x2", 0), ("downy", 3),
-    ("x1", 1), ("x3", 0), ("x2", 1), ("x1", 2), ("y2", 1), ("y1", 2), ("y3", 0), ("w", 0), ("gx1", 0), ("x3", 1),
-    ("x1", 3), ("y1", 3), ("x2", 2), ("y3", 1), ("gx2", 0), ("y2", 2), ("gy1", 0), ("gx1", 1), ("gy1", 1),
-    ("gx3", 0), ("x3", 2), ("y2", 3), ("gy2", 0), ("w", 1), ("x2", 3), ("gx2", 1), ("y3", 2), ("gy2", 1),
-    ("gy3", 0), ("x3", 3), ("y3", 3), ("o", 0), ("mma", 0), ("mm", 0), ("gy1", 2), ("gx1", 2), ("gx3", 1),
-    ("gy3", 1), ("mma", 1), ("gx1", 3), ("o", 1), ("gy1", 3), ("gx2", 2), ("gy2", 2), ("mm", 1), ("gx2", 3),
-    ("gy2", 3), ("gx3", 2), ("gy3", 2), ("z1", 0), ("mma", 2), ("gx3", 3), ("gy3", 3), ("o", 2), ("mm", 2),
-    ("mma", 3), ("mm", 3), ("o", 3), ("z1", 1), ("out", 0), ("out", 1), ("out", 2), ("o", 4), ("out", 3),
+    ("lam", 0), ("lam", 1), ("downx", 0), ("downy", 0), ("lam", 2), ("downx", 1), ("downy", 1), ("y1", 0),
+    ("downx", 2), ("downy", 2), ("lam", 3), ("x1", 0), ("y2", 0), ("y1", 1), ("x1", 1), ("downx", 3), ("x2", 0),
+    ("y1", 2), ("x1", 2), ("downy", 3), ("x3", 0), ("x2", 1), ("y2", 2), ("y2", 1), ("x2", 2), ("x1", 3),
+    ("x3", 1), ("x3", 2), ("y3", 2), ("w", 0), ("gx1", 0), ("y3", 0), ("y1", 3), ("x2", 3), ("gx1", 2), ("gy1", 2),
+    ("y3", 1), ("x3", 3), ("gy1", 0), ("y2", 3), ("gx1", 1), ("w", 1), ("gy1", 1), ("gx2", 2), ("gx2", 1),
+    ("gy2", 2), ("gy2", 0), ("gx2", 0), ("y3", 3), ("o", 0), ("gx3", 2), ("gy3", 2), ("gy2", 1), ("gx1", 3),
+    ("o", 1), ("mma", 2), ("gx3", 0), ("gy1", 3), ("gy3", 0), ("mm", 2), ("mma", 0), ("gy3", 1), ("mm", 0),
+    ("gx3", 1), ("mma", 1), ("gy3", 3), ("mm", 1), ("gx3", 3), ("o", 2), ("mma", 3), ("mm", 3), ("o", 3),
+    ("out", 2), ("out", 0), ("out", 1), ("o", 4), ("out", 3),
 )
-STRAIGHT = (2, 3)
-SPREAD = ()
+STRAIGHT = (0, 1, 2, 3)
+SPREAD = (3,)
 
 
 def kernel(

time: 83.4 us -> 83.8 us (level)
  no operation moved by 1% of the time
where the time goes in v5:
time: 83.8 us; the launch traced here: 82.8 us
  Pallas kernels  82.2 us (98%)
    pallas_call x1, Pallas kernels, per_device(): pl.pallas_call(kernel, name='bound_pass', out_shape=(jax.ShapeDtypeStruct...  80.5 us

profile of v5, /device:TPU:0, one launch (start us, length us, event | category | flops | bytes accessed | tf_op | source)
XLA Modules:
  0.0 82.8 jit_solution(16050777839608229747)
XLA Ops:
  0.6 80.5 %bound_pass.1 = (f32[128,512]{1,0:T(8,128)}, f32[1,64]{1,0:T(1,128)}) custom-call(s32[2,1024]{1,0:T(2,128)} %bitcast.12, bf16[2048,512]{1,0:T(8,128)(2,1)} %readout.1, bf16[512,3584]{1,0:T(8,128)(2,1)} %gate.1, bf16[512,3584]{1,0:T(8,128)(2,1)} %up.1, bf16[3584,512]{1,0:T(8,128)(2,1)} %down.1, f32[28,128]{1,0:T(8,128)} %bitcast.7, f32[28,128]{1,0:T(8,128)} %bitcast.8, ...), custom_call_target="tpu_custom_call" | custom-call | tf_op jit(solution)/shard_map/bound_pass/pallas_call | solution.py:533
  81.1 1.7 %hand_over.1 = (f32[128,512]{1,0:T(8,128)}, f32[1,64]{1,0:T(1,128)}) custom-call(f32[128,512]{1,0:T(8,128)} %get-tuple-element.6.coeffs, f32[1,64]{1,0:T(1,128)} %get-tuple-element.7.offsets), custom_call_target="tpu_custom_call" | custom-call | tf_op jit(solution)/shard_map/hand_over/pallas_call | solution.py:547
